TPU v7x, 128 devices: a whole 4x4x4 slice. The times are simulated.
128 devices in a mesh: img: 8 (over z, core), tile: 16 (over x, y).
Axes of the slice: x: 4, y: 4, z: 4, core: 2. Of those that a mesh axis runs over, the one named last changes fastest.
Arguments:
- features: bfloat16 [256, 2400, 256], P(('img', 'tile')), may hold values from -6 to 6
- cluster_ids: int32 [256, 4, 2400], P(('img', 'tile')), may hold values from 0 to 63
- soft_weights: bfloat16 [256, 4, 2400], P(('img', 'tile')), may hold values from 0.019897461 to 1
- counts: int32 [256], P(('img', 'tile')), may hold values from 600 to 2400, as said below
- centroids: bfloat16 [64, 256], replicated, may hold values from -3 to 3
- covariance: float32 [16384, 16384], P('img', 'tile'), may hold values from -1.5 to 1.5
Outputs:
- updated: float32 [16384, 16384], P('img', 'tile')
Inputs may be any that keep to these rules, and one draw needn't show every extreme that they name: `counts`: some image has exactly 2400 valid features and some exactly 600.
All inputs are finite; a program needn't handle non-finite values.
Results may differ from a plain program's by a relative error of at most 0.0003.
Values sent between devices are 32-bit elements; how exact they have to be, the bound alone decides.
A program may use at most 64 MiB of HBM per device.

v0:
```python
import jax
import jax.numpy as jnp
from jax import lax
from jax.sharding import PartitionSpec as P


def aggregate(features, cluster_ids, soft_weights, counts, centroids):
    img_dev, top_count, max_slots = cluster_ids.shape
    cluster_count = centroids.shape[0]
    labels = lax.broadcasted_iota(jnp.int32, (1, cluster_count, 1), 1)
    assign = jnp.zeros((img_dev, cluster_count, max_slots), jnp.float32)
    for slot in range(top_count):
        matched = cluster_ids[:, slot : slot + 1, :] == labels
        assign = assign + jnp.where(
            matched, soft_weights[:, slot : slot + 1, :].astype(jnp.float32), 0.0
        )
    in_range = lax.broadcasted_iota(jnp.int32, (1, 1, max_slots), 2) < counts[:, None, None]
    assign = jnp.where(in_range, assign, 0.0).astype(jnp.bfloat16)
    weight_sum = jnp.sum(assign, axis=2, dtype=jnp.float32)
    residual = jnp.einsum("ikf,ifc->ikc", assign, features, preferred_element_type=jnp.float32)
    residual = residual - weight_sum[:, :, None] * centroids.astype(jnp.float32)[None, :, :]
    magnitude = jnp.sqrt(jnp.sum(residual * residual, axis=2, keepdims=True) + 1e-06)
    return (residual / magnitude).reshape(img_dev, -1)


def outer_block(left_rows, right_rows):
    return lax.dot_general(
        left_rows,
        right_rows,
        (((0,), (0,)), ((), ())),
        precision=lax.Precision.HIGHEST,
        preferred_element_type=jnp.float32,
    )


def body(features, cluster_ids, soft_weights, counts, centroids, covariance):
    vlad_rows = aggregate(features, cluster_ids, soft_weights, counts, centroids)
    img_shards = lax.axis_size("img")
    tile_shards = lax.axis_size("tile")
    img_dev = vlad_rows.shape[0]
    width_rows = covariance.shape[0]
    width_cols = covariance.shape[1]
    factor = float(centroids.shape[1]) / float(img_dev * img_shards * tile_shards)
    row_part = vlad_rows.reshape(img_dev, img_shards, 1, width_rows).transpose(1, 2, 0, 3)
    row_part = jnp.broadcast_to(row_part, (img_shards, tile_shards, img_dev, width_rows))
    col_part = vlad_rows.reshape(img_dev, 1, tile_shards, width_cols).transpose(1, 2, 0, 3)
    col_part = jnp.broadcast_to(col_part, (img_shards, tile_shards, img_dev, width_cols))
    outgoing = jnp.concatenate((row_part, col_part), axis=3)
    outgoing = outgoing.reshape(img_shards * tile_shards * img_dev, width_rows + width_cols)
    incoming = lax.all_to_all(outgoing, ("img", "tile"), split_axis=0, concat_axis=0, tiled=True)
    product = outer_block(incoming[:, :width_rows], incoming[:, width_rows:])
    return covariance + factor * product


def solution(mesh):
    return jax.shard_map(
        body,
        mesh=mesh,
        in_specs=(
            P(("img", "tile"), None, None),
            P(("img", "tile"), None, None),
            P(("img", "tile"), None, None),
            P(("img", "tile")),
            P(),
            P("img", "tile"),
        ),
        out_specs=P("img", "tile"),
        check_vma=False,
    )
```

profile of v0, /device:TPU:0, one launch (start us, length us, event | category | flops | bytes accessed | tf_op | source)
XLA Modules:
  0.0 78.2 jit_solution(1189851186298516498)
XLA Ops:
  0.0 0.0 copy-start
  0.0 0.9 %iota_compare_fusion.4 = pred[2,2400]{1,0:T(4,128)(4,1)S(1)} fusion(s32[2]{0:T(128)} %param.9), kind=kLoop, calls=%fused_computation.25 | loop fusion | flops 4800 | bytes 4808 | tf_op jit(solution)/shard_map/lt | solution.py:17
  0.9 0.8 convert_element_type.15
  1.7 1.2 %fusion.3 = (s32[2,1,2400]{2,1,0:T(1,128)S(1)}, s32[2,1,2400]{2,1,0:T(1,128)S(1)}, s32[2,1,2400]{2,1,0:T(1,128)S(1)}, s32[2,1,2400]{2,1,0:T(1,128)S(1)}) fusion(s32[2,4,2400]{2,1,0:T(4,128)} %param.7), kind=kLoop, calls=%fused_computation.28 | loop fusion | bytes 153600 | tf_op jit(solution)/shard_map/slice | solution.py:13
  2.8 1.0 %slice_convert_fusion.3 = (f32[2,1,2400]{2,1,0:T(1,128)S(1)}, f32[2,1,2400]{2,1,0:T(1,128)S(1)}, f32[2,1,2400]{2,1,0:T(1,128)S(1)}, f32[2,1,2400]{2,1,0:T(1,128)S(1)}) fusion(bf16[2,4,2400]{2,1,0:T(4,128)(2,1)} %param.8), kind=kLoop, calls=%fused_computation.24 | loop fusion | flops 19200 | bytes 115200 | tf_op jit(solution)/shard_map/jit(_where)/broadcast_in_dim | solution.py:14
  3.9 1.0 %convert_reduce_fusion = f32[2,64]{1,0:T(2,128)S(1)} fusion(f32[2,2400]{1,0:T(2,128)S(1)} %get-tuple-element.15, s32[2,2400]{1,0:T(2,128)S(1)} %get-tuple-element.19, f32[2,2400]{1,0:T(2,128)S(1)} %get-tuple-element.16, s32[2,2400]{1,0:T(2,128)S(1)} %get-tuple-element.20, f32[2,2400]{1,0:T(2,128)S(1)} %get-tuple-element.17, ...), kind=kLoop, calls=%fused_computation.3 | loop fusion | flops 4607872 | bytes 158912 | tf_op jit(solution)/shard_map/reduce_sum | solution.py:19
  5.0 0.0 copy-done
  5.0 1.0 %multiply_reduce_fusion = (f32[2,64]{1,0:T(2,128)S(1)}, f32[2,64,256]{2,1,0:T(8,128)S(1)}) fusion(f32[64,256]{1,0:T(8,128)S(1)} %convert_element_type.15, f32[2,64]{1,0:T(2,128)S(1)} %convert_reduce_fusion, bf16[2,2400,256]{2,1,0:T(8,128)(2,1)S(1)} %copy-done, f32[2,2400]{1,0:T(2,128)S(1)} %get-tuple-element.15, s32[2,2400]{1,0:T(2,128)S(1)} %get-tuple-element.19, ...), kind=kOutput, calls=%fused_computation.11 | convolution fusion | flops 161410944 | bytes 2813632 | tf_op jit(solution)/shard_map/ikf,ifc->ikc/dot_general | solution.py:20
  6.0 0.1 broadcast_divide_fusion
  6.2 0.1 copy.9
  6.3 0.1 copy.10
  6.4 0.3 broadcast_in_dim.95
  6.8 1.0 %broadcast_in_dim.93 = f32[8,16,2,2048]{3,2,1,0:T(2,128)S(1)} broadcast(f32[8,2,2048]{2,1,0:T(2,128)S(1)} %copy.9), dimensions={0,2,3} | broadcast | bytes 2228224 | tf_op jit(solution)/shard_map/broadcast_in_dim | solution.py:45
  7.8 1.7 %pad_maximum_fusion = f32[8,16,2,3072]{3,2,1,0:T(2,128)S(1)} fusion(f32[8,16,2,1024]{3,2,1,0:T(2,128)S(1)} %broadcast_in_dim.95, f32[8,16,2,2048]{3,2,1,0:T(2,128)S(1)} %broadcast_in_dim.93), kind=kLoop, calls=%fused_computation.1 | loop fusion | flops 786432 | bytes 6291456 | tf_op jit(solution)/shard_map/concatenate | solution.py:48
  9.5 51.5 %all_to_all.12 = f32[128,2,3072]{2,1,0:T(2,128)} all-to-all(f32[128,2,3072]{2,1,0:T(2,128)S(1)} %bitcast.24), channel_id=1, replica_groups=mesh['img'=8,'tile'=16] {'img','tile'}, dimensions={0} | all-to-all | bytes 6291456 | tf_op jit(solution)/shard_map/all_to_all | solution.py:50
  61.0 5.3 %all_to_all.10 = f32[256,3072]{1,0:T(8,128)} reshape(f32[128,2,3072]{2,1,0:T(2,128)} %all_to_all.12) | data formatting | bytes 6291456 | tf_op jit(solution)/shard_map/all_to_all | solution.py:50
  66.2 11.9 %convolution_add_fusion = f32[2048,1024]{1,0:T(8,128)} fusion(f32[2048,1024]{1,0:T(8,128)} %param.11, f32[256,3072]{1,0:T(8,128)} %all_to_all.10), kind=kOutput, calls=%fused_computation | convolution fusion | flops 6444548096 | bytes 19922944 | tf_op jit(solution)/shard_map/dot_general | solution.py:27
  (7 shorter events, 0.2 us)
Async XLA Ops:
  0.0 5.0 %copy-start = (bf16[2,2400,256]{2,1,0:T(8,128)(2,1)S(1)}, bf16[2,2400,256]{2,1,0:T(8,128)(2,1)}, u32[]{:S(2)}) copy-start(bf16[2,2400,256]{2,1,0:T(8,128)(2,1)} %param.6) | copy-start | bytes 7372804
where the time goes:
time: 79.4 us; the launch traced here: 78.2 us
  blocking collectives  51.5 us (65%)
  matrix products  12.9 us (16%)
  local copies, waits for them, and re-layouts  8.16 us (10%)
  other arithmetic  5.43 us (7%)
    all_to_all x1, blocking collectives, body(): lax.all_to_all(outgoing, ('img', 'tile'), split_axis=0, concat_axis=0, ti...  51.5 us
    dot_general x1, matrix products, outer_block(): lax.dot_general(left_rows, right_rows, (((0,), (0,)), ((), ())), precisio...  11.9 us
    all_to_all x1, local copies, waits for them, and re-layouts, body(): lax.all_to_all(outgoing, ('img', 'tile'), split_axis=0, concat_axis=0, ti...  5.26 us
    concatenate x1, other arithmetic, body(): outgoing = jnp.concatenate((row_part, col_part), axis=3)  1.65 us

commit v1 on v0

v1 whole, which is shorter than its diff:
```python
import functools

import jax
import jax.numpy as jnp
from jax import lax
from jax.experimental import pallas as pl
from jax.experimental.pallas import tpu as pltpu
from jax.sharding import PartitionSpec as P

MESH = pl.DeviceIdType.MESH
CLUSTERS, DESC, TOPK, IMAGES = 64, 256, 4, 256
SIDE = 4
ROWS = 8
COLS = 4
LANES = 128


def vlad_kernel(counts, features, ids, weights, centroids, rows):
    image = pl.program_id(0)
    slots = ids.shape[2]
    labels = lax.broadcasted_iota(jnp.int32, (CLUSTERS, 1), 0)
    in_range = lax.broadcasted_iota(jnp.int32, (1, slots), 1) < counts[image]
    assign = jnp.zeros((CLUSTERS, slots), jnp.float32)
    for slot in range(TOPK):
        weight = jnp.where(in_range, weights[0, slot : slot + 1, :].astype(jnp.float32), 0.0)
        assign = assign + jnp.where(ids[0, slot : slot + 1, :] == labels, weight, 0.0)
    assign = assign.astype(jnp.bfloat16)
    weight_sum = jnp.sum(assign.astype(jnp.float32), axis=1, keepdims=True)
    residual = jnp.dot(assign, features[0], preferred_element_type=jnp.float32)
    residual = residual - weight_sum * centroids[...].astype(jnp.float32)
    magnitude = jnp.sqrt(jnp.sum(residual * residual, axis=1, keepdims=True) + 1e-06)
    residual = residual / magnitude
    for block in range(CLUSTERS // ROWS):
        for half in range(DESC // LANES):
            rows[0, block, half] = residual[
                block * ROWS : (block + 1) * ROWS, half * LANES : (half + 1) * LANES
            ]


def gather_kernel(vlad, left, right, cols, send_sem, recv_sem, own_sem):
    img, tile = lax.axis_index("img"), lax.axis_index("tile")
    z, core, x, y = img // 2, img % 2, tile // SIDE, tile % SIDE

    def at(dx, dy, dz, dc):
        return (
            lax.rem(z + dz + SIDE, SIDE) * 2 + lax.rem(core + dc, 2),
            lax.rem(x + dx + SIDE, SIDE) * SIDE + lax.rem(y + dy + SIDE, SIDE),
        )

    column = [(0, 0, dz, dc) for dz in range(SIDE) for dc in range(2) if dz or dc]
    plane = [(dx, dy, 0, 0) for dx in range(SIDE) for dy in range(SIDE) if dx or dy]
    barrier = pltpu.get_barrier_semaphore()
    for step in column + plane:
        pl.semaphore_signal(barrier, inc=1, device_id=at(*step), device_id_type=MESH)

    for block in range(CLUSTERS // COLS):
        for k in range(2):
            for half in range(DESC // LANES):
                start = k * ROWS + half * COLS
                first_row = block * COLS % ROWS
                cols[block, start : start + COLS] = vlad[
                    k, block * COLS // ROWS, half, first_row : first_row + COLS
                ]
    pl.semaphore_wait(barrier, len(column + plane))

    copies = []

    def put(source, target, step):
        index = len(copies)
        copy = pltpu.make_async_remote_copy(
            src_ref=source,
            dst_ref=target,
            send_sem=send_sem.at[index],
            recv_sem=recv_sem.at[index],
            device_id=at(*step),
            device_id_type=MESH,
        )
        copy.start()
        copies.append(copy)
        return copy

    def block_of(index):
        return vlad.at[:, index]

    own_left = pltpu.make_async_copy(block_of(img), left.at[tile, img], own_sem.at[0])
    own_left.start()
    own_right = pltpu.make_async_copy(cols.at[tile], right.at[tile, img], own_sem.at[1])
    own_right.start()
    blocks = [put(block_of(at(*step)[0]), left.at[tile, img], step) for step in column]
    parts = [put(cols.at[at(*step)[1]], right.at[tile, img], step) for step in plane]
    own_left.wait()
    for copy in blocks:
        copy.wait_recv()

    forward, backward = ((1, 0), (0, 1)), ((-1, 0), (0, -1))

    def part(dx, dy, start, size):
        index = at(dx, dy, 0, 0)[1]
        return left.at[index, pl.ds(start, size)]

    def send(half, dx, dy, start, size, axis, sign):
        step = [0, 0, 0, 0]
        step[axis] = sign
        ref = part(dx, dy, start, size)
        return put(ref, ref, step)

    first = {}
    for half in (0, 1):
        for sign in (1, -1):
            first[half, sign] = send(half, 0, 0, 4 * half, 4, half, sign)
    second = {}
    for half in (0, 1):
        for sign in (1, -1):
            second[half, 0, sign] = send(half, 0, 0, 4 * half, 4, 1 - half, sign)

    def along(half, distance, across):
        return (distance, across) if half == 0 else (across, distance)

    relay = {}
    for half in (0, 1):
        for sign in (1, -1):
            first[half, sign].wait_recv()
            start = 4 * half + (0 if sign == 1 else 2)
            dx, dy = along(half, -sign, 0)
            relay[half, sign] = send(half, dx, dy, start, 2, half, sign)

    own_right.wait()
    for copy in parts:
        copy.wait_recv()

    def slab(dz):
        return right.at[:, at(0, 0, dz, 0)[0]]

    def half_slab(dz, top):
        return right.at[pl.ds(8 * top, 8), at(0, 0, dz, 0)[0]]

    up = put(slab(0), slab(0), (0, 0, 1, 0))
    down = put(slab(0), slab(0), (0, 0, -1, 0))
    twins = [put(slab(0), slab(0), (0, 0, 0, 1))]

    for half in (0, 1):
        for sign in (1, -1):
            dx, dy = along(half, -sign, 0)
            for turn in (1, -1):
                second[half, -sign, turn] = send(half, dx, dy, 4 * half, 4, 1 - half, turn)

    late = {}

    def hop(half, distance):
        for turn in (1, -1):
            second[half, distance, turn].wait_recv()
            dx, dy = along(half, distance, -turn)
            start = 4 * half + (0 if turn == 1 else 2)
            late[half, distance, turn] = send(half, dx, dy, start, 2, 1 - half, turn)

    for half in (0, 1):
        hop(half, 0)
    for half in (0, 1):
        for sign in (1, -1):
            relay[half, sign].wait_recv()
        dx, dy = along(half, 2, 0)
        for turn in (1, -1):
            second[half, 2, turn] = send(half, dx, dy, 4 * half, 4, 1 - half, turn)

    up.wait_recv()
    up2 = put(half_slab(-1, 0), half_slab(-1, 0), (0, 0, 1, 0))
    twins.append(put(slab(-1), slab(-1), (0, 0, 0, 1)))
    down.wait_recv()
    down2 = put(half_slab(1, 1), half_slab(1, 1), (0, 0, -1, 0))
    twins.append(put(slab(1), slab(1), (0, 0, 0, 1)))

    for distance in (1, -1):
        for half in (0, 1):
            hop(half, distance)
    up2.wait_recv()
    down2.wait_recv()
    twins.append(put(slab(2), slab(2), (0, 0, 0, 1)))
    for half in (0, 1):
        hop(half, 2)
    for copy in twins:
        copy.wait_recv()
    for copy in late.values():
        copy.wait_recv()
    for copy in copies:
        copy.wait_send()


def product_kernel(left, right, covariance, updated, high, low):
    k = pl.program_id(0)

    def split(value):
        top = value.astype(jnp.bfloat16)
        return top, (value - top.astype(jnp.float32)).astype(jnp.bfloat16)

    def cluster(ref, index, count):
        return jnp.concatenate(
            [ref[pl.ds(half * count + index, IMAGES, stride=2 * count), :] for half in range(2)], axis=1
        )

    @pl.when(k == 0)
    def _():
        for j in range(COLS):
            top, rest = split(cluster(right, j, COLS))
            high[:, j * DESC : (j + 1) * DESC] = top
            low[:, j * DESC : (j + 1) * DESC] = rest

    top, rest = split(cluster(left, k, ROWS))
    dot = functools.partial(
        lax.dot_general, dimension_numbers=(((0,), (0,)), ((), ())), preferred_element_type=jnp.float32
    )
    updated[...] = covariance[...] + (dot(top, high[...]) + (dot(rest, high[...]) + dot(top, low[...])))


def body(features, cluster_ids, soft_weights, counts, centroids, covariance):
    images, slots, _ = features.shape
    height, width = covariance.shape
    vmem = pl.BlockSpec(memory_space=pltpu.VMEM)
    vlad = pl.pallas_call(
        vlad_kernel,
        grid=(images,),
        in_specs=[
            pl.BlockSpec(memory_space=pltpu.SMEM),
            pl.BlockSpec((1, slots, DESC), lambda i: (i, 0, 0)),
            pl.BlockSpec((1, TOPK, slots), lambda i: (i, 0, 0)),
            pl.BlockSpec((1, TOPK, slots), lambda i: (i, 0, 0)),
            pl.BlockSpec((CLUSTERS, DESC), lambda i: (0, 0)),
        ],
        out_specs=pl.BlockSpec((1, CLUSTERS // ROWS, 2, ROWS, LANES), lambda i: (i, 0, 0, 0, 0)),
        out_shape=jax.ShapeDtypeStruct((images, CLUSTERS // ROWS, 2, ROWS, LANES), jnp.float32),
        compiler_params=pltpu.CompilerParams(vmem_limit_bytes=32 * 2**20),
        name="vlad",
    )(counts, features, cluster_ids, soft_weights, centroids)
    n_copies = 7 + 15 + 8 + 4 + 12 + 16 + 4 + 4 + 4
    left, right = pl.pallas_call(
        gather_kernel,
        in_specs=[vmem],
        out_specs=[vmem, vmem],
        out_shape=[
            jax.ShapeDtypeStruct((16, 8, images, 2, ROWS, LANES), jnp.float32),
            jax.ShapeDtypeStruct((16, 8, images * 2 * COLS, LANES), jnp.float32),
        ],
        scratch_shapes=[
            pltpu.VMEM((16, images * 2 * COLS, LANES), jnp.float32),
            pltpu.SemaphoreType.DMA((n_copies,)),
            pltpu.SemaphoreType.DMA((n_copies,)),
            pltpu.SemaphoreType.DMA((2,)),
        ],
        compiler_params=pltpu.CompilerParams(
            collective_id=0, has_side_effects=True, vmem_limit_bytes=32 * 2**20
        ),
        name="gather",
    )(vlad)
    return pl.pallas_call(
        product_kernel,
        grid=(height // DESC,),
        in_specs=[vmem, vmem, pl.BlockSpec((DESC, width), lambda k: (k, 0))],
        out_specs=pl.BlockSpec((DESC, width), lambda k: (k, 0)),
        out_shape=jax.ShapeDtypeStruct((height, width), jnp.float32),
        scratch_shapes=[pltpu.VMEM((IMAGES, width), jnp.bfloat16)] * 2,
        compiler_params=pltpu.CompilerParams(vmem_limit_bytes=32 * 2**20),
        name="product",
    )(left.reshape(-1, LANES), right.reshape(-1, LANES), covariance)


def solution(mesh):
    return jax.shard_map(
        body,
        mesh=mesh,
        in_specs=(
            P(("img", "tile"), None, None),
            P(("img", "tile"), None, None),
            P(("img", "tile"), None, None),
            P(("img", "tile")),
            P(),
            P("img", "tile"),
        ),
        out_specs=P("img", "tile"),
        check_vma=False,
    )
```

time: 79.4 us -> 47.1 us (0.59); the launches traced: 78.2 us -> 46.7 us
  blocking collectives: 51.5 us -> 0 us
  Pallas kernels: 0 us -> 38.5 us
  matrix products: 12.9 us -> 0 us
  other arithmetic: 5.43 us -> 0 us
    all_to_all x1 -> x0, blocking collectives: 51.5 us -> none  [body(): lax.all_to_all(outgoing, ('img', 'tile'), split_axis=0, concat_axis=0, ti...]
    pallas_call x0 -> x3, Pallas kernels: none -> 38.5 us  [the longest x1 29.2 us: body(): pl.pallas_call(gather_kernel, in_specs=[vmem], out_specs=[vmem, vmem], ou...]
    dot_general x2 -> x0, matrix products: 12.9 us -> none  [the longest x1 11.9 us: outer_block(): lax.dot_general(left_rows, right_rows, (((0,), (0,)), ((), ())), precisio...]
    unnamed x6 -> x12, local copies, waits for them, and re-layouts: 0.09 us -> 8.14 us
    all_to_all x1 -> x0, local copies, waits for them, and re-layouts: 5.26 us -> none  [body(): lax.all_to_all(outgoing, ('img', 'tile'), split_axis=0, concat_axis=0, ti...]
    concatenate x1 -> x0, other arithmetic: 1.65 us -> none  [body(): outgoing = jnp.concatenate((row_part, col_part), axis=3)]
    broadcast_in_dim x4 -> x0, local copies, waits for them, and re-layouts: 1.59 us -> none  [the longest x2 1.14 us: body(): jnp.broadcast_to(row_part, (img_shards, tile_shards, img_dev, width_rows))]
    slice x1 -> x0, local copies, waits for them, and re-layouts: 1.15 us -> none  [aggregate(): matched = cluster_ids[:, slot:slot + 1, :] == labels]
where the time goes in v1:
time: 47.1 us; the launch traced here: 46.7 us
  Pallas kernels  38.5 us (82%)
  local copies, waits for them, and re-layouts  8.14 us (17%)
    pallas_call x1, Pallas kernels, body(): pl.pallas_call(gather_kernel, in_specs=[vmem], out_specs=[vmem, vmem], ou...  29.2 us
    unnamed x12, local copies, waits for them, and re-layouts  8.14 us
    pallas_call x1, Pallas kernels, body(): pl.pallas_call(product_kernel, grid=(height // DESC,), in_specs=[vmem, vm...  7.58 us
    pallas_call x1, Pallas kernels, body(): pl.pallas_call(vlad_kernel, grid=(images,), in_specs=[pl.BlockSpec(memory...  1.73 us

profile of v1, /device:TPU:0, one launch (start us, length us, event | category | flops | bytes accessed | tf_op | source)
XLA Modules:
  0.0 46.7 jit_solution(6969321449031576098)
XLA Ops:
  0.0 0.0 copy-start.1
  0.0 1.7 %copy-done.1 = bf16[2,2400,256]{2,1,0:T(8,128)(2,1)S(1)} copy-done((bf16[2,2400,256]{2,1,0:T(8,128)(2,1)S(1)}, bf16[2,2400,256]{2,1,0:T(8,128)(2,1)}, u32[]{:S(2)}) %copy-start.1) | copy-done | bytes 2457624
  1.7 0.0 copy-start.2
  1.7 0.9 %copy-done.2 = s32[2,4,2400]{2,1,0:T(4,128)S(1)} copy-done((s32[2,4,2400]{2,1,0:T(4,128)S(1)}, s32[2,4,2400]{2,1,0:T(4,128)}, u32[]{:S(2)}) %copy-start.2) | copy-done | bytes 76824
  2.6 0.0 copy-start.3
  2.6 0.8 %copy-done.3 = bf16[2,4,2400]{2,1,0:T(4,128)(2,1)S(1)} copy-done((bf16[2,4,2400]{2,1,0:T(4,128)(2,1)S(1)}, bf16[2,4,2400]{2,1,0:T(4,128)(2,1)}, u32[]{:S(2)}) %copy-start.3) | copy-done | bytes 38424
  3.4 0.0 copy-start.4
  3.4 0.8 %copy-done.4 = bf16[64,256]{1,0:T(8,128)(2,1)S(1)} copy-done((bf16[64,256]{1,0:T(8,128)(2,1)S(1)}, bf16[64,256]{1,0:T(8,128)(2,1)}, u32[]{:S(2)}) %copy-start.4) | copy-done | bytes 32792
  4.1 0.0 copy-start.5
  4.1 0.7 %copy-done.5 = s32[2]{0:T(128)S(1)} copy-done((s32[2]{0:T(128)S(1)}, s32[2]{0:T(128)}, u32[]{:S(2)}) %copy-start.5) | copy-done | bytes 32
  4.8 1.7 %vlad.1 = f32[2,8,2,8,128]{4,3,2,1,0:T(8,128)S(1)} custom-call(s32[2]{0:T(128)S(1)} %copy-done.5, bf16[2,2400,256]{2,1,0:T(8,128)(2,1)S(1)} %copy-done.1, s32[2,4,2400]{2,1,0:T(4,128)S(1)} %copy-done.2, bf16[2,4,2400]{2,1,0:T(4,128)(2,1)S(1)} %copy-done.3, bf16[64,256]{1,0:T(8,128)(2,1)S(1)} %copy-done.4), custom_call_target="tpu_custom_call" | custom-call | tf_op jit(solution)/shard_map/vlad/pallas_call | solution.py:218
  6.5 29.2 %gather.1 = (f32[16,8,2,2,8,128]{5,4,3,2,1,0:T(8,128)S(1)}, f32[16,8,16,128]{3,2,1,0:T(8,128)S(1)}) custom-call(f32[2,8,2,8,128]{4,3,2,1,0:T(8,128)S(1)} %vlad.1), custom_call_target="tpu_custom_call" | custom-call | tf_op jit(solution)/shard_map/gather/pallas_call | solution.py:234
  35.7 0.0 copy-start
  35.8 3.4 %copy-done = f32[2048,1024]{1,0:T(8,128)S(1)} copy-done((f32[2048,1024]{1,0:T(8,128)S(1)}, f32[2048,1024]{1,0:T(8,128)}, u32[]{:S(2)}) %copy-start) | copy-done | bytes 8388632
  39.1 7.6 %product.1 = f32[2048,1024]{1,0:T(8,128)} custom-call(f32[4096,128]{1,0:T(8,128)S(1)} %bitcast.2, f32[2048,128]{1,0:T(8,128)S(1)} %bitcast.3, f32[2048,1024]{1,0:T(8,128)S(1)} %copy-done), custom_call_target="tpu_custom_call" | custom-call | tf_op jit(solution)/shard_map/product/pallas_call | solution.py:253
Async XLA Ops:
  0.0 1.7 %copy-start.1 = (bf16[2,2400,256]{2,1,0:T(8,128)(2,1)S(1)}, bf16[2,2400,256]{2,1,0:T(8,128)(2,1)}, u32[]{:S(2)}) copy-start(bf16[2,2400,256]{2,1,0:T(8,128)(2,1)} %features.1) | copy-start | bytes 7372804
  1.7 0.9 %copy-start.2 = (s32[2,4,2400]{2,1,0:T(4,128)S(1)}, s32[2,4,2400]{2,1,0:T(4,128)}, u32[]{:S(2)}) copy-start(s32[2,4,2400]{2,1,0:T(4,128)} %ids.1) | copy-start | bytes 230404
  2.6 0.8 %copy-start.3 = (bf16[2,4,2400]{2,1,0:T(4,128)(2,1)S(1)}, bf16[2,4,2400]{2,1,0:T(4,128)(2,1)}, u32[]{:S(2)}) copy-start(bf16[2,4,2400]{2,1,0:T(4,128)(2,1)} %weights.1) | copy-start | bytes 115204
  3.4 0.8 %copy-start.4 = (bf16[64,256]{1,0:T(8,128)(2,1)S(1)}, bf16[64,256]{1,0:T(8,128)(2,1)}, u32[]{:S(2)}) copy-start(bf16[64,256]{1,0:T(8,128)(2,1)} %centroids.1) | copy-start | bytes 98308
  4.1 0.7 %copy-start.5 = (s32[2]{0:T(128)S(1)}, s32[2]{0:T(128)}, u32[]{:S(2)}) copy-start(s32[2]{0:T(128)} %counts.1) | copy-start | bytes 28
  35.7 3.4 %copy-start = (f32[2048,1024]{1,0:T(8,128)S(1)}, f32[2048,1024]{1,0:T(8,128)}, u32[]{:S(2)}) copy-start(f32[2048,1024]{1,0:T(8,128)} %covariance.1) | copy-start | bytes 25165828

commit v2 on v0

v2 whole, which is shorter than its diff:
```python
import jax
import jax.numpy as jnp
from jax import lax
from jax.experimental import pallas as pl
from jax.experimental.pallas import tpu as pltpu
from jax.sharding import PartitionSpec as P

MESH = pl.DeviceIdType.MESH
CLUSTERS, DESC, TOPK, IMAGES = 64, 256, 4, 256
SIDE = 4
ROWS = 8
COLS = 4
LANES = 128
PLACE = {0: 0, -1: 1, 1: 2, 2: 3}
BACK = {0: 0, -1: 1, 1: -1, 2: 2}
GROUPS = {0: (0, 8), 1: (8, 16), 2: (24, 8)}


def gather_kernel(
    counts, features, ids, weights, centroids, covariance,
    left, right, total,
    count_s, feature_v, id_v, weight_v, centroid_v, vlad, cols,
    load_sem, cov_sem, own_sem,
    first_send, first_recv, next_send, next_recv, relay_send, relay_recv, col_send, col_recv,
):
    img, tile = lax.axis_index("img"), lax.axis_index("tile")
    z, core, x, y = img // 2, img % 2, tile // SIDE, tile % SIDE

    def at(dx, dy, dz, dc):
        return (
            lax.rem(z + dz + SIDE, SIDE) * 2 + lax.rem(core + dc, 2),
            lax.rem(x + dx + SIDE, SIDE) * SIDE + lax.rem(y + dy + SIDE, SIDE),
        )

    loads = [[], []]
    loads[0].append(pltpu.make_async_copy(counts, count_s, load_sem.at[0]))
    loads[0].append(pltpu.make_async_copy(centroids, centroid_v, load_sem.at[1]))
    for k in range(2):
        for n, (source, target) in enumerate(((ids, id_v), (weights, weight_v), (features, feature_v))):
            loads[k].append(pltpu.make_async_copy(source.at[k], target.at[k], load_sem.at[2 + 3 * k + n]))
    for copy in loads[0] + loads[1]:
        copy.start()

    distances = (2, 1, -1, 0)
    plane = [(dx, dy, 0, 0) for dx in distances for dy in distances if dx or dy]
    peers = list(plane)
    for d in distances:
        for dz in distances:
            for dc in range(2):
                if dz or dc:
                    peers += [(d, 0, dz, dc)] + ([(0, d, dz, dc)] if d else [])
    barrier = pltpu.get_barrier_semaphore()
    for step in peers:
        pl.semaphore_signal(barrier, inc=1, device_id=at(*step), device_id_type=MESH)
    fill = pltpu.make_async_copy(covariance, total, cov_sem.at[0])
    fill.start()

    def aggregate(k):
        for copy in loads[k]:
            copy.wait()
        slots = id_v.shape[2]
        labels = lax.broadcasted_iota(jnp.int32, (CLUSTERS, 1), 0)
        in_range = lax.broadcasted_iota(jnp.int32, (1, slots), 1) < count_s[k]
        assign = jnp.zeros((CLUSTERS, slots), jnp.float32)
        for slot in range(TOPK):
            weight = jnp.where(in_range, weight_v[k, slot : slot + 1, :].astype(jnp.float32), 0.0)
            assign = assign + jnp.where(id_v[k, slot : slot + 1, :] == labels, weight, 0.0)
        assign = assign.astype(jnp.bfloat16)
        weight_sum = jnp.sum(assign.astype(jnp.float32), axis=1, keepdims=True)
        residual = jnp.dot(assign, feature_v[k], preferred_element_type=jnp.float32)
        residual = residual - weight_sum * centroid_v[...].astype(jnp.float32)
        magnitude = jnp.sqrt(jnp.sum(residual * residual, axis=1, keepdims=True) + 1e-06)
        residual = residual / magnitude
        for half in range(2):
            lanes = slice(half * LANES, (half + 1) * LANES)
            for block in range(CLUSTERS // ROWS):
                vlad[k, block, half] = residual[block * ROWS : (block + 1) * ROWS, lanes]
            for block in range(CLUSTERS // COLS):
                start = k * 2 * COLS + half * COLS
                cols[block, start : start + COLS] = residual[block * COLS : (block + 1) * COLS, lanes]

    sent = []

    def put(source, target, send_sem, recv_sem, step):
        copy = pltpu.make_async_remote_copy(
            src_ref=source, dst_ref=target, send_sem=send_sem, recv_sem=recv_sem,
            device_id=at(*step), device_id_type=MESH,
        )
        copy.start()
        return copy

    def group_of(distance):
        return abs(distance)

    def along(k, first, second):
        return (first, second, 0, 0) if k == 0 else (second, first, 0, 0)

    def exchange(k):
        own = pltpu.make_async_copy(vlad.at[k, img], left.at[k, 0, 0], own_sem.at[k])
        own.start()
        for d in (0, 2, 1, -1):
            for dz in (2, 1, -1, 0):
                for dc in range(2):
                    if d or dz or dc:
                        step = along(k, d, 0)[:2] + (dz, dc)
                        slot = PLACE[BACK[d]] * 8 + PLACE[BACK[dz]] * 2 + dc
                        put(
                            vlad.at[k, at(*step)[0]], left.at[k, 0, slot],
                            first_send.at[k], first_recv.at[k, group_of(d)], step,
                        )
        return own

    def arrived(ref, sem):
        pltpu.make_async_copy(ref, ref, sem).wait()

    aggregate(0)
    pl.semaphore_wait(barrier, len(peers))
    own = [exchange(0)]
    aggregate(1)
    own.append(exchange(1))
    own_cols = pltpu.make_async_copy(cols.at[tile], right.at[0, 0], own_sem.at[2])
    own_cols.start()
    for step in plane:
        slot = PLACE[BACK[step[0]]] * SIDE + PLACE[BACK[step[1]]]
        put(cols.at[at(*step)[1]], right.at[slot, 0], col_send.at[0], col_recv.at[0], step)

    onward = {}

    def second(k, group):
        start, size = GROUPS[group]
        if group == 0:
            own[k].wait()
            arrived(left.at[k, 0, pl.ds(1, 7)], first_recv.at[k, 0])
        else:
            arrived(left.at[k, 0, pl.ds(start, size)], first_recv.at[k, group])
        slots = pl.ds(start, size)
        for n, turn in enumerate((1, -1)):
            onward[k, group, turn] = put(
                left.at[k, 0, slots], left.at[k, PLACE[-turn], slots],
                next_send.at[k, group, n], next_recv.at[k, group, n], along(k, 0, turn),
            )
            sent.append(onward[k, group, turn])

    relays = []

    def relay(k, group):
        start, size = GROUPS[group]
        for n, turn in enumerate((1, -1)):
            onward[k, group, turn].wait_recv()
            slots = pl.ds(start + n * size // 2, size // 2)
            relays.append(
                put(
                    left.at[k, PLACE[-turn], slots], left.at[k, PLACE[2], slots],
                    relay_send.at[k, group, n], relay_recv.at[k, group, n], along(k, 0, turn),
                )
            )

    second(0, 0)
    second(1, 0)
    second(0, 1)
    second(1, 1)
    own_cols.wait()
    arrived(right.at[pl.ds(1, 15), 0], col_recv.at[0])

    def slab(dz, dc):
        return right.at[:, PLACE[dz] * 2 + dc]

    def twin(dz):
        n = 4 + PLACE[dz]
        return put(slab(dz, 0), slab(dz, 1), col_send.at[n], col_recv.at[n], (0, 0, 0, 1))

    spread = [
        put(slab(0, 0), slab(BACK[dz], 0), col_send.at[PLACE[dz]], col_recv.at[PLACE[dz]], (0, 0, dz, 0))
        for dz in (2, 1, -1)
    ]
    twins = [twin(0)]
    second(0, 2)
    second(1, 2)
    relay(0, 0)
    relay(1, 0)
    for copy, dz in zip(spread, (2, -1, 1)):
        copy.wait_recv()
        twins.append(twin(dz))
    relay(0, 1)
    relay(1, 1)
    for k in range(2):
        arrived(left.at[k, 0, pl.ds(1, 31)], first_send.at[k])
    arrived(cols.at[pl.ds(1, 15)], col_send.at[0])
    relay(0, 2)
    relay(1, 2)
    fill.wait()
    for copy in twins:
        copy.wait_recv()
    for copy in spread + twins + sent:
        copy.wait_send()
    for copy in relays:
        copy.wait()


def product_kernel(left, right, total, updated, factor):
    k = pl.program_id(0)

    def split(value):
        top = value.astype(jnp.bfloat16)
        return top, (value - top.astype(jnp.float32)).astype(jnp.bfloat16)

    @pl.when(k == 0)
    def _():
        for j in range(COLS):
            pieces = []
            for image in range(2):
                for second in range(SIDE):
                    for first in range(SIDE):
                        dx, dy = (first, second) if image == 0 else (second, first)
                        base = (dx * SIDE + dy) * 8 * 16 + image * 8 + j
                        pieces.append(
                            jnp.concatenate(
                                [right[pl.ds(base + 4 * half, 8, stride=16), :] for half in range(2)], axis=1
                            )
                        )
            top, rest = split(jnp.concatenate(pieces, axis=0))
            columns = slice(j * DESC, (j + 1) * DESC)
            factor[:IMAGES, columns] = top
            factor[IMAGES : 2 * IMAGES, columns] = top
            factor[2 * IMAGES :, columns] = rest

    top, rest = split(
        jnp.concatenate([left[pl.ds(half * ROWS + k, IMAGES, stride=2 * ROWS), :] for half in range(2)], axis=1)
    )
    updated[...] = total[pl.ds(pl.multiple_of(k * DESC, DESC), DESC), :] + lax.dot_general(
        jnp.concatenate([top, rest, top], axis=0),
        factor[...],
        (((0,), (0,)), ((), ())),
        preferred_element_type=jnp.float32,
    )


def body(features, cluster_ids, soft_weights, counts, centroids, covariance):
    images, slots, _ = features.shape
    height, width = covariance.shape
    vmem = pl.BlockSpec(memory_space=pltpu.VMEM)
    hbm = pl.BlockSpec(memory_space=pltpu.HBM)
    dma = pltpu.SemaphoreType.DMA
    left, right, total = pl.pallas_call(
        gather_kernel,
        in_specs=[hbm] * 6,
        out_specs=[vmem] * 3,
        out_shape=[
            jax.ShapeDtypeStruct((images, SIDE, 32, 2, ROWS, LANES), jnp.float32),
            jax.ShapeDtypeStruct((16, 8, images * 2 * COLS, LANES), jnp.float32),
            jax.ShapeDtypeStruct((height, width), jnp.float32),
        ],
        scratch_shapes=[
            pltpu.SMEM((images,), jnp.int32),
            pltpu.VMEM(features.shape, features.dtype),
            pltpu.VMEM(cluster_ids.shape, cluster_ids.dtype),
            pltpu.VMEM(soft_weights.shape, soft_weights.dtype),
            pltpu.VMEM(centroids.shape, centroids.dtype),
            pltpu.VMEM((images, CLUSTERS // ROWS, 2, ROWS, LANES), jnp.float32),
            pltpu.VMEM((16, images * 2 * COLS, LANES), jnp.float32),
            dma((8,)), dma((1,)), dma((3,)),
            dma((2,)), dma((2, 3)), dma((2, 3, 2)), dma((2, 3, 2)), dma((2, 3, 2)), dma((2, 3, 2)),
            dma((8,)), dma((8,)),
        ],
        compiler_params=pltpu.CompilerParams(
            collective_id=0, has_side_effects=True, vmem_limit_bytes=32 * 2**20
        ),
        name="gather",
    )(*(
        pltpu.with_memory_space_constraint(value, pltpu.HBM)
        for value in (counts, features, cluster_ids, soft_weights, centroids, covariance)
    ))
    return pl.pallas_call(
        product_kernel,
        grid=(height // DESC,),
        in_specs=[vmem] * 3,
        out_specs=pl.BlockSpec((DESC, width), lambda k: (k, 0)),
        out_shape=jax.ShapeDtypeStruct((height, width), jnp.float32),
        scratch_shapes=[pltpu.VMEM((3 * IMAGES, width), jnp.bfloat16)],
        compiler_params=pltpu.CompilerParams(vmem_limit_bytes=32 * 2**20),
        name="product",
    )(left.reshape(-1, LANES), right.reshape(-1, LANES), total)


def solution(mesh):
    return jax.shard_map(
        body,
        mesh=mesh,
        in_specs=(
            P(("img", "tile"), None, None),
            P(("img", "tile"), None, None),
            P(("img", "tile"), None, None),
            P(("img", "tile")),
            P(),
            P("img", "tile"),
        ),
        out_specs=P("img", "tile"),
        check_vma=False,
    )
```

time: 79.4 us -> 38.3 us (0.48); the launches traced: 78.2 us -> 37.9 us
  blocking collectives: 51.5 us -> 0 us
  Pallas kernels: 0 us -> 37.9 us
  matrix products: 12.9 us -> 0 us
  local copies, waits for them, and re-layouts: 8.16 us -> 0 us
  other arithmetic: 5.43 us -> 0 us
    all_to_all x1 -> x0, blocking collectives: 51.5 us -> none  [body(): lax.all_to_all(outgoing, ('img', 'tile'), split_axis=0, concat_axis=0, ti...]
    pallas_call x0 -> x2, Pallas kernels: none -> 37.9 us  [the longest x1 30.1 us: body(): pl.pallas_call(gather_kernel, in_specs=[hbm] * 6, out_specs=[vmem] * 3, o...]
    dot_general x2 -> x0, matrix products: 12.9 us -> none  [the longest x1 11.9 us: outer_block(): lax.dot_general(left_rows, right_rows, (((0,), (0,)), ((), ())), precisio...]
    all_to_all x1 -> x0, local copies, waits for them, and re-layouts: 5.26 us -> none  [body(): lax.all_to_all(outgoing, ('img', 'tile'), split_axis=0, concat_axis=0, ti...]
    concatenate x1 -> x0, other arithmetic: 1.65 us -> none  [body(): outgoing = jnp.concatenate((row_part, col_part), axis=3)]
    broadcast_in_dim x4 -> x0, local copies, waits for them, and re-layouts: 1.59 us -> none  [the longest x2 1.14 us: body(): jnp.broadcast_to(row_part, (img_shards, tile_shards, img_dev, width_rows))]
    slice x1 -> x0, local copies, waits for them, and re-layouts: 1.15 us -> none  [aggregate(): matched = cluster_ids[:, slot:slot + 1, :] == labels]
    reduce_sum x1 -> x0, other arithmetic: 1.02 us -> none  [aggregate(): weight_sum = jnp.sum(assign, axis=2, dtype=jnp.float32)]
where the time goes in v2:
time: 38.3 us; the launch traced here: 37.9 us
  Pallas kernels  37.9 us (99%)
    pallas_call x1, Pallas kernels, body(): pl.pallas_call(gather_kernel, in_specs=[hbm] * 6, out_specs=[vmem] * 3, o...  30.1 us
    pallas_call x1, Pallas kernels, body(): pl.pallas_call(product_kernel, grid=(height // DESC,), in_specs=[vmem] *...  7.79 us

profile of v2, /device:TPU:0, one launch (start us, length us, event | category | flops | bytes accessed | tf_op | source)
XLA Modules:
  0.0 37.9 jit_solution(14494570170557372292)
XLA Ops:
  0.0 30.1 %gather.1 = (f32[2,4,32,2,8,128]{5,4,3,2,1,0:T(8,128)S(1)}, f32[16,8,16,128]{3,2,1,0:T(8,128)S(1)}, f32[2048,1024]{1,0:T(8,128)S(1)}) custom-call(s32[2]{0:T(128)} %counts.1, bf16[2,2400,256]{2,1,0:T(8,128)(2,1)} %features.1, s32[2,4,2400]{2,1,0:T(4,128)} %ids.1, bf16[2,4,2400]{2,1,0:T(4,128)(2,1)} %weights.1, bf16[64,256]{1,0:T(8,128)(2,1)} %centroids.1, ...), custom_call_target="tpu_custom_call" | custom-call | tf_op jit(solution)/shard_map/gather/pallas_call | solution.py:244
  30.1 7.8 %product.1 = f32[2048,1024]{1,0:T(8,128)} custom-call(f32[4096,128]{1,0:T(8,128)S(1)} %bitcast.2, f32[2048,128]{1,0:T(8,128)S(1)} %bitcast.3, f32[2048,1024]{1,0:T(8,128)S(1)} %get-tuple-element.10.total), custom_call_target="tpu_custom_call" | custom-call | tf_op jit(solution)/shard_map/product/pallas_call | solution.py:273

commit v3 on v2

v3 whole, which is shorter than its diff:
```python
import jax
import jax.numpy as jnp
from jax import lax
from jax.experimental import pallas as pl
from jax.experimental.pallas import tpu as pltpu
from jax.sharding import PartitionSpec as P

MESH = pl.DeviceIdType.MESH
CLUSTERS, DESC, TOPK, IMAGES = 64, 256, 4, 256
SIDE = 4
ROWS = 8
COLS = 4
LANES = 128
PLACE = {0: 0, -1: 1, 1: 2, 2: 3}
BACK = {0: 0, -1: 1, 1: -1, 2: 2}
DIMS = (((0,), (0,)), ((), ()))


def split(value):
    top = value.astype(jnp.bfloat16)
    return top, (value - top.astype(jnp.float32)).astype(jnp.bfloat16)


def columns_of(right, v):
    blocks = []
    for j in range(COLS):
        halves = []
        for half in range(2):
            halves.append(
                jnp.concatenate(
                    [
                        right[pl.ds((zc * SIDE + v) * 64 + half * COLS + j, 8, stride=8), :]
                        for zc in range(8)
                    ],
                    axis=0,
                )
            )
        blocks.append(jnp.concatenate(halves, axis=1))
    top, rest = split(jnp.concatenate(blocks, axis=1))
    return top, rest


def rows_of(left, start, count, k):
    top, rest = split(
        jnp.concatenate(
            [left[pl.ds(start * 16 + half * ROWS + k, count, stride=16), :] for half in range(2)], axis=1
        )
    )
    return jnp.concatenate([top, rest, top], axis=0)


def gather_kernel(
    counts, features, ids, weights, centroids, covariance,
    left, right, total,
    count_s, feature_v, id_v, weight_v, centroid_v, vlad, cols, factor,
    load_sem, cov_sem, z_send, z_recv, u_send, u_recv, v_send, v_recv, r_send, r_recv,
    c_send, c_recv, s_send, s_recv,
):
    img, tile = lax.axis_index("img"), lax.axis_index("tile")
    z, core, x, y = img // 2, img % 2, tile // SIDE, tile % SIDE

    def at(dx, dy, dz, dc):
        return (
            lax.rem(z + dz + SIDE, SIDE) * 2 + lax.rem(core + dc, 2),
            lax.rem(x + dx + SIDE, SIDE) * SIDE + lax.rem(y + dy + SIDE, SIDE),
        )

    loads = [[], []]
    loads[0].append(pltpu.make_async_copy(counts, count_s, load_sem.at[0]))
    loads[0].append(pltpu.make_async_copy(centroids, centroid_v, load_sem.at[1]))
    for k in range(2):
        for n, (source, target) in enumerate(((ids, id_v), (weights, weight_v), (features, feature_v))):
            loads[k].append(pltpu.make_async_copy(source.at[k], target.at[k], load_sem.at[2 + 3 * k + n]))
    for copy in loads[0] + loads[1]:
        copy.start()

    distances = (2, 1, -1, 0)
    plane = [(dx, dy, 0, 0) for dx in distances for dy in distances if dx or dy]
    column = [(0, 0, dz, dc) for dz in distances for dc in (1, 0) if dz or dc]
    barrier = pltpu.get_barrier_semaphore()
    for step in plane + column:
        pl.semaphore_signal(barrier, inc=1, device_id=at(*step), device_id_type=MESH)
    fill = pltpu.make_async_copy(covariance, total, cov_sem.at[0])
    fill.start()

    def aggregate(k):
        for copy in loads[k]:
            copy.wait()
        slots = id_v.shape[2]
        labels = lax.broadcasted_iota(jnp.int32, (CLUSTERS, 1), 0)
        in_range = lax.broadcasted_iota(jnp.int32, (1, slots), 1) < count_s[k]
        assign = jnp.zeros((CLUSTERS, slots), jnp.float32)
        for slot in range(TOPK):
            weight = jnp.where(in_range, weight_v[k, slot : slot + 1, :].astype(jnp.float32), 0.0)
            assign = assign + jnp.where(id_v[k, slot : slot + 1, :] == labels, weight, 0.0)
        assign = assign.astype(jnp.bfloat16)
        weight_sum = jnp.sum(assign.astype(jnp.float32), axis=1, keepdims=True)
        residual = jnp.dot(assign, feature_v[k], preferred_element_type=jnp.float32)
        residual = residual - weight_sum * centroid_v[...].astype(jnp.float32)
        magnitude = jnp.sqrt(jnp.sum(residual * residual, axis=1, keepdims=True) + 1e-06)
        residual = residual / magnitude
        for half in range(2):
            lanes = slice(half * LANES, (half + 1) * LANES)
            for block in range(CLUSTERS // ROWS):
                vlad[k, block, half] = residual[block * ROWS : (block + 1) * ROWS, lanes]
            for block in range(CLUSTERS // COLS):
                cols[block, k, half * COLS : (half + 1) * COLS] = residual[block * COLS : (block + 1) * COLS, lanes]

    def put(source, target, send_sem, recv_sem, step):
        copy = pltpu.make_async_remote_copy(
            src_ref=source, dst_ref=target, send_sem=send_sem, recv_sem=recv_sem,
            device_id=at(*step), device_id_type=MESH,
        )
        copy.start()
        return copy

    def wait(ref, sem):
        pltpu.make_async_copy(ref, ref, sem).wait()

    def along(k, u, v):
        return (u, v, 0, 0) if k == 0 else (v, u, 0, 0)

    def column_pieces(k):
        pltpu.make_async_copy(cols.at[tile, k], right.at[0, 0, 0, k, 0], c_recv.at[0]).start()
        for step in plane:
            u, v = step[:2] if k == 0 else (step[1], step[0])
            target = right.at[0, 0, PLACE[BACK[v]], k, PLACE[BACK[u]]]
            put(cols.at[at(*step)[1], k], target, c_send.at[0], c_recv.at[0], step)

    def row_pieces(k):
        pltpu.make_async_copy(vlad.at[k, img], left.at[0, 0, 0, k, 0], z_recv.at[k, 0]).start()
        for step in column:
            n = PLACE[BACK[step[2]]]
            put(vlad.at[k, at(*step)[0]], left.at[0, n, step[3], k, 0], z_send.at[k], z_recv.at[k, n], step)

    def go_u(k, j):
        wait(left.at[0, j, :, k, 0], z_recv.at[k, j])
        for u in (2, 1, -1):
            target = left.at[0, j, :, k, PLACE[BACK[u]]]
            put(left.at[0, j, :, k, 0], target, u_send.at[k], u_recv.at[k, j], along(k, u, 0))

    onward = {}

    def go_v(k, j):
        wait(left.at[0, j, :, k, pl.ds(1, 3)], u_recv.at[k, j])
        for n, turn in enumerate((1, -1)):
            target = left.at[PLACE[-turn], j, :, k]
            onward[k, j, n] = put(
                left.at[0, j, :, k], target, v_send.at[k], v_recv.at[k, j, n], along(k, 0, turn)
            )

    def relay(k, j):
        for n, turn in enumerate((1, -1)):
            onward[k, j, n].wait_recv()
            source = left.at[PLACE[-turn], j, :, k, pl.ds(2 * n, 2)]
            target = left.at[PLACE[2], j, :, k, pl.ds(2 * n, 2)]
            put(source, target, r_send.at[k], r_recv.at[k], along(k, 0, turn))

    def twin(dz):
        n = PLACE[dz]
        return put(right.at[n, 0], right.at[n, 1], s_send.at[n + 4], s_recv.at[n + 4], (0, 0, 0, 1))

    aggregate(0)
    pl.semaphore_wait(barrier, len(plane + column))
    column_pieces(0)
    row_pieces(0)
    aggregate(1)
    column_pieces(1)
    row_pieces(1)
    for j in range(SIDE):
        for k in range(2):
            go_u(k, j)
    wait(right.at[0, 0], c_recv.at[0])
    spread = {
        dz: put(
            right.at[0, 0], right.at[PLACE[BACK[dz]], 0], s_send.at[PLACE[dz]], s_recv.at[PLACE[dz]],
            (0, 0, dz, 0),
        )
        for dz in (2, 1, -1)
    }
    twins = [twin(0)]
    for j in range(2):
        for k in range(2):
            go_v(k, j)
    for k in range(2):
        go_v(k, 2)
    for k in range(2):
        relay(k, 0)
    for dz in (1, -1):
        spread[dz].wait_recv()
        twins.append(twin(BACK[dz]))
    for k in range(2):
        go_v(k, 3)
    for k in range(2):
        relay(k, 1)
    spread[2].wait_recv()
    twins.append(twin(2))
    for k in range(2):
        relay(k, 2)
    for k in range(2):
        relay(k, 3)
    for copy in twins:
        copy.wait_recv()

    flat_right = right.reshape(-1, LANES)
    flat_left = left.reshape(-1, LANES)
    for v in range(SIDE - 1):
        top, rest = columns_of(flat_right, v)
        factor[v * 64 : (v + 1) * 64] = top
        factor[192 + v * 64 : 192 + (v + 1) * 64] = top
        factor[384 + v * 64 : 384 + (v + 1) * 64] = rest
    fill.wait()
    for k in range(ROWS):
        total[k * DESC : (k + 1) * DESC] += lax.dot_general(
            rows_of(flat_left, 0, 192, k), factor[...], DIMS, preferred_element_type=jnp.float32
        )

    wait(cols.at[pl.ds(0, 15)], c_send.at[0])
    for copy in list(spread.values()) + twins:
        copy.wait_send()
    for k in range(2):
        wait(vlad.at[k, pl.ds(0, 7)], z_send.at[k])
        wait(left.at[0, :, :, k, pl.ds(1, 3)], u_send.at[k])
        wait(left.at[pl.ds(1, 2), :, :, k], v_send.at[k])
        wait(left.at[3, :, :, k], r_send.at[k])
        wait(left.at[3, :, :, k], r_recv.at[k])


def product_kernel(left, right, total, updated, staged, factor, sems):
    top, rest = columns_of(right, SIDE - 1)
    factor[:64] = top
    factor[64:128] = top
    factor[128:] = rest
    copies = []
    for k in range(ROWS):
        rows = slice(k * DESC, (k + 1) * DESC)
        staged[rows] = total[rows] + lax.dot_general(
            rows_of(left, 192, 64, k), factor[...], DIMS, preferred_element_type=jnp.float32
        )
        copies.append(pltpu.make_async_copy(staged.at[rows], updated.at[rows], sems.at[k]))
        copies[-1].start()
    for copy in copies:
        copy.wait()


def body(features, cluster_ids, soft_weights, counts, centroids, covariance):
    images = features.shape[0]
    height, width = covariance.shape
    vmem = pl.BlockSpec(memory_space=pltpu.VMEM)
    hbm = pl.BlockSpec(memory_space=pltpu.HBM)
    dma = pltpu.SemaphoreType.DMA
    operands = (counts, features, cluster_ids, soft_weights, centroids, covariance)
    left, right, total = pl.pallas_call(
        gather_kernel,
        in_specs=[hbm] * 6,
        out_specs=[vmem] * 3,
        out_shape=[
            jax.ShapeDtypeStruct((SIDE, SIDE, 2, images, SIDE, 2, ROWS, LANES), jnp.float32),
            jax.ShapeDtypeStruct((SIDE, 2, SIDE, images, SIDE, 2 * COLS, LANES), jnp.float32),
            jax.ShapeDtypeStruct((height, width), jnp.float32),
        ],
        scratch_shapes=[
            pltpu.SMEM((images,), jnp.int32),
            pltpu.VMEM(features.shape, features.dtype),
            pltpu.VMEM(cluster_ids.shape, cluster_ids.dtype),
            pltpu.VMEM(soft_weights.shape, soft_weights.dtype),
            pltpu.VMEM(centroids.shape, centroids.dtype),
            pltpu.VMEM((images, CLUSTERS // ROWS, 2, ROWS, LANES), jnp.float32),
            pltpu.VMEM((16, images, 2 * COLS, LANES), jnp.float32),
            pltpu.VMEM((3 * 192, width), jnp.bfloat16),
            dma((8,)), dma((1,)), dma((2,)), dma((2, 4)), dma((2,)), dma((2, 4)),
            dma((2,)), dma((2, 4, 2)), dma((2,)), dma((2,)), dma((1,)), dma((1,)), dma((8,)), dma((8,)),
        ],
        compiler_params=pltpu.CompilerParams(
            collective_id=0, has_side_effects=True, vmem_limit_bytes=32 * 2**20
        ),
        name="gather",
    )(*(pltpu.with_memory_space_constraint(value, pltpu.HBM) for value in operands))
    return pl.pallas_call(
        product_kernel,
        in_specs=[vmem] * 3,
        out_specs=hbm,
        out_shape=jax.ShapeDtypeStruct((height, width), jnp.float32),
        scratch_shapes=[
            pltpu.VMEM((height, width), jnp.float32),
            pltpu.VMEM((192, width), jnp.bfloat16),
            dma((ROWS,)),
        ],
        compiler_params=pltpu.CompilerParams(vmem_limit_bytes=32 * 2**20),
        name="product",
    )(left.reshape(-1, LANES), right.reshape(-1, LANES), total)


def solution(mesh):
    return jax.shard_map(
        body,
        mesh=mesh,
        in_specs=(
            P(("img", "tile"), None, None),
            P(("img", "tile"), None, None),
            P(("img", "tile"), None, None),
            P(("img", "tile")),
            P(),
            P("img", "tile"),
        ),
        out_specs=P("img", "tile"),
        check_vma=False,
    )
```

time: 38.3 us -> 33 us (0.86)
  Pallas kernels: 37.9 us -> 32.8 us
    pallas_call x1, Pallas kernels: 7.79 us -> 3.7 us  [body(): pl.pallas_call(product_kernel, in_specs=[vmem] * 3, out_specs=hbm, out_sh...]
    pallas_call x1, Pallas kernels: 30.1 us -> 29.1 us  [body(): pl.pallas_call(gather_kernel, in_specs=[hbm] * 6, out_specs=[vmem] * 3, o...]
where the time goes in v3:
time: 33 us; the launch traced here: 32.9 us
  Pallas kernels  32.8 us (99%)
    pallas_call x1, Pallas kernels, body(): pl.pallas_call(gather_kernel, in_specs=[hbm] * 6, out_specs=[vmem] * 3, o...  29.1 us
    pallas_call x1, Pallas kernels, body(): pl.pallas_call(product_kernel, in_specs=[vmem] * 3, out_specs=hbm, out_sh...  3.7 us

profile of v3, /device:TPU:0, one launch (start us, length us, event | category | flops | bytes accessed | tf_op | source)
XLA Modules:
  0.0 32.9 jit_solution(6750485698997447165)
XLA Ops:
  0.0 29.1 %gather.1 = (f32[4,4,2,2,4,2,8,128]{7,6,5,4,3,2,1,0:T(8,128)S(1)}, f32[4,2,4,2,4,8,128]{6,5,4,3,2,1,0:T(8,128)S(1)}, f32[2048,1024]{1,0:T(8,128)S(1)}) custom-call(s32[2]{0:T(128)} %counts.1, bf16[2,2400,256]{2,1,0:T(8,128)(2,1)} %features.1, s32[2,4,2400]{2,1,0:T(4,128)} %ids.1, bf16[2,4,2400]{2,1,0:T(4,128)(2,1)} %weights.1, bf16[64,256]{1,0:T(8,128)(2,1)} %centroids.1, ...), custom_call_target="tpu_custom_call" | custom-call | tf_op jit(solution)/shard_map/gather/pallas_call | solution.py:253
  29.2 3.7 %product.1 = f32[2048,1024]{1,0:T(8,128)} custom-call(f32[4096,128]{1,0:T(8,128)S(1)} %bitcast.2, f32[2048,128]{1,0:T(8,128)S(1)} %bitcast.3, f32[2048,1024]{1,0:T(8,128)S(1)} %get-tuple-element.10.total), custom_call_target="tpu_custom_call" | custom-call | tf_op jit(solution)/shard_map/product/pallas_call | solution.py:279

commit v4 on v3

--- a/solution.py
+++ b/solution.py
@@ -167,9 +167,14 @@
     aggregate(1)
     column_pieces(1)
     row_pieces(1)
-    for j in range(SIDE):
-        for k in range(2):
-            go_u(k, j)
+    for k in range(2):
+        go_u(k, 0)
+    for k in range(2):
+        go_u(k, 1)
+    for k in range(2):
+        go_u(k, 2)
+    for k in range(2):
+        go_u(k, 3)
     wait(right.at[0, 0], c_recv.at[0])
     spread = {
         dz: put(
@@ -179,18 +184,19 @@
         for dz in (2, 1, -1)
     }
     twins = [twin(0)]
-    for j in range(2):
-        for k in range(2):
-            go_v(k, j)
+    for k in range(2):
+        go_v(k, 0)
+    for k in range(2):
+        go_v(k, 1)
     for k in range(2):
         go_v(k, 2)
     for k in range(2):
-        relay(k, 0)
+        go_v(k, 3)
     for dz in (1, -1):
         spread[dz].wait_recv()
         twins.append(twin(BACK[dz]))
     for k in range(2):
-        go_v(k, 3)
+        relay(k, 0)
     for k in range(2):
         relay(k, 1)
     spread[2].wait_recv()

time: 33 us -> 31.2 us (0.945)
  Pallas kernels: 32.8 us -> 30.7 us
    pallas_call x1, Pallas kernels: 29.1 us -> 27 us  [body(): pl.pallas_call(gather_kernel, in_specs=[hbm] * 6, out_specs=[vmem] * 3, o...]
where the time goes in v4:
time: 31.2 us; the launch traced here: 30.7 us
  Pallas kernels  30.7 us (98%)
    pallas_call x1, Pallas kernels, body(): pl.pallas_call(gather_kernel, in_specs=[hbm] * 6, out_specs=[vmem] * 3, o...  27 us
    pallas_call x1, Pallas kernels, body(): pl.pallas_call(product_kernel, in_specs=[vmem] * 3, out_specs=hbm, out_sh...  3.7 us

profile of v4, /device:TPU:0, one launch (start us, length us, event | category | flops | bytes accessed | tf_op | source)
XLA Modules:
  0.0 30.7 jit_solution(11281817036881621069)
XLA Ops:
  0.0 27.0 %gather.1 = (f32[4,4,2,2,4,2,8,128]{7,6,5,4,3,2,1,0:T(8,128)S(1)}, f32[4,2,4,2,4,8,128]{6,5,4,3,2,1,0:T(8,128)S(1)}, f32[2048,1024]{1,0:T(8,128)S(1)}) custom-call(s32[2]{0:T(128)} %counts.1, bf16[2,2400,256]{2,1,0:T(8,128)(2,1)} %features.1, s32[2,4,2400]{2,1,0:T(4,128)} %ids.1, bf16[2,4,2400]{2,1,0:T(4,128)(2,1)} %weights.1, bf16[64,256]{1,0:T(8,128)(2,1)} %centroids.1, ...), custom_call_target="tpu_custom_call" | custom-call | tf_op jit(solution)/shard_map/gather/pallas_call | solution.py:259
  27.0 3.7 %product.1 = f32[2048,1024]{1,0:T(8,128)} custom-call(f32[4096,128]{1,0:T(8,128)S(1)} %bitcast.2, f32[2048,128]{1,0:T(8,128)S(1)} %bitcast.3, f32[2048,1024]{1,0:T(8,128)S(1)} %get-tuple-element.10.total), custom_call_target="tpu_custom_call" | custom-call | tf_op jit(solution)/shard_map/product/pallas_call | solution.py:285

commit v5 on v4

--- a/solution.py
+++ b/solution.py
@@ -51,8 +51,8 @@
 
 def gather_kernel(
     counts, features, ids, weights, centroids, covariance,
-    left, right, total,
-    count_s, feature_v, id_v, weight_v, centroid_v, vlad, cols, factor,
+    left, right, total, spare_rows, spare_columns,
+    count_s, feature_v, id_v, weight_v, centroid_v, vlad, cols, factor, stacked,
     load_sem, cov_sem, z_send, z_recv, u_send, u_recv, v_send, v_recv, r_send, r_recv,
     c_send, c_recv, s_send, s_recv,
 ):
@@ -160,6 +160,37 @@
         n = PLACE[dz]
         return put(right.at[n, 0], right.at[n, 1], s_send.at[n + 4], s_recv.at[n + 4], (0, 0, 0, 1))
 
+    flat_right = right.reshape(-1, LANES)
+    flat_left = left.reshape(-1, LANES)
+
+    def stack_rows(v):
+        for k in range(ROWS):
+            values = [flat_left[pl.ds(v * 1024 + half * ROWS + k, 64, stride=16), :] for half in range(2)]
+            top, rest = split(jnp.concatenate(values, axis=1))
+            stacked[k, v * 64 : (v + 1) * 64] = top
+            stacked[k, 192 + v * 64 : 192 + (v + 1) * 64] = rest
+            if v < 2:
+                stacked[k, 384 + v * 64 : 384 + (v + 1) * 64] = top
+            else:
+                spare_rows[k] = top
+
+    def stack_columns(j):
+        for v in range(SIDE - 1):
+            blocks = []
+            for k in range(COLS):
+                for half in range(2):
+                    start = (2 * j * SIDE + v) * 64 + half * COLS + k
+                    pieces = [flat_right[pl.ds(start + core * 256, 8, stride=8), :] for core in range(2)]
+                    blocks.append(jnp.concatenate(pieces, axis=0))
+            top, rest = split(jnp.concatenate(blocks, axis=1))
+            start = v * 64 + j * 16
+            factor[start : start + 16] = top
+            factor[192 + start : 192 + start + 16] = top
+            if v < 2:
+                factor[384 + start : 384 + start + 16] = rest
+            else:
+                spare_columns[j * 16 : (j + 1) * 16] = rest
+
     aggregate(0)
     pl.semaphore_wait(barrier, len(plane + column))
     column_pieces(0)
@@ -192,6 +223,7 @@
         go_v(k, 2)
     for k in range(2):
         go_v(k, 3)
+    stack_rows(0)
     for dz in (1, -1):
         spread[dz].wait_recv()
         twins.append(twin(BACK[dz]))
@@ -205,20 +237,20 @@
         relay(k, 2)
     for k in range(2):
         relay(k, 3)
-    for copy in twins:
-        copy.wait_recv()
-
-    flat_right = right.reshape(-1, LANES)
-    flat_left = left.reshape(-1, LANES)
-    for v in range(SIDE - 1):
-        top, rest = columns_of(flat_right, v)
-        factor[v * 64 : (v + 1) * 64] = top
-        factor[192 + v * 64 : 192 + (v + 1) * 64] = top
-        factor[384 + v * 64 : 384 + (v + 1) * 64] = rest
+    twins[0].wait_recv()
+    stack_columns(0)
+    twins[1].wait_recv()
+    stack_columns(1)
+    twins[2].wait_recv()
+    stack_columns(2)
+    stack_rows(1)
+    stack_rows(2)
+    twins[3].wait_recv()
+    stack_columns(3)
     fill.wait()
     for k in range(ROWS):
         total[k * DESC : (k + 1) * DESC] += lax.dot_general(
-            rows_of(flat_left, 0, 192, k), factor[...], DIMS, preferred_element_type=jnp.float32
+            stacked[k], factor[...], DIMS, preferred_element_type=jnp.float32
         )
 
     wait(cols.at[pl.ds(0, 15)], c_send.at[0])
@@ -232,16 +264,20 @@
         wait(left.at[3, :, :, k], r_recv.at[k])
 
 
-def product_kernel(left, right, total, updated, staged, factor, sems):
+def product_kernel(left, right, total, spare_rows, spare_columns, updated, staged, factor, sems):
     top, rest = columns_of(right, SIDE - 1)
     factor[:64] = top
     factor[64:128] = top
-    factor[128:] = rest
+    factor[128:192] = rest
+    factor[192:] = spare_columns[...]
     copies = []
     for k in range(ROWS):
         rows = slice(k * DESC, (k + 1) * DESC)
         staged[rows] = total[rows] + lax.dot_general(
-            rows_of(left, 192, 64, k), factor[...], DIMS, preferred_element_type=jnp.float32
+            jnp.concatenate([rows_of(left, 192, 64, k), spare_rows[k]], axis=0),
+            factor[...],
+            DIMS,
+            preferred_element_type=jnp.float32,
         )
         copies.append(pltpu.make_async_copy(staged.at[rows], updated.at[rows], sems.at[k]))
         copies[-1].start()
@@ -256,14 +292,16 @@
     hbm = pl.BlockSpec(memory_space=pltpu.HBM)
     dma = pltpu.SemaphoreType.DMA
     operands = (counts, features, cluster_ids, soft_weights, centroids, covariance)
-    left, right, total = pl.pallas_call(
+    left, right, *rest = pl.pallas_call(
         gather_kernel,
         in_specs=[hbm] * 6,
-        out_specs=[vmem] * 3,
+        out_specs=[vmem] * 5,
         out_shape=[
             jax.ShapeDtypeStruct((SIDE, SIDE, 2, images, SIDE, 2, ROWS, LANES), jnp.float32),
             jax.ShapeDtypeStruct((SIDE, 2, SIDE, images, SIDE, 2 * COLS, LANES), jnp.float32),
             jax.ShapeDtypeStruct((height, width), jnp.float32),
+            jax.ShapeDtypeStruct((ROWS, 64, DESC), jnp.bfloat16),
+            jax.ShapeDtypeStruct((64, width), jnp.bfloat16),
         ],
         scratch_shapes=[
             pltpu.SMEM((images,), jnp.int32),
@@ -273,7 +311,8 @@
             pltpu.VMEM(centroids.shape, centroids.dtype),
             pltpu.VMEM((images, CLUSTERS // ROWS, 2, ROWS, LANES), jnp.float32),
             pltpu.VMEM((16, images, 2 * COLS, LANES), jnp.float32),
-            pltpu.VMEM((3 * 192, width), jnp.bfloat16),
+            pltpu.VMEM((512, width), jnp.bfloat16),
+            pltpu.VMEM((ROWS, 512, DESC), jnp.bfloat16),
             dma((8,)), dma((1,)), dma((2,)), dma((2, 4)), dma((2,)), dma((2, 4)),
             dma((2,)), dma((2, 4, 2)), dma((2,)), dma((2,)), dma((1,)), dma((1,)), dma((8,)), dma((8,)),
         ],
@@ -284,17 +323,17 @@
     )(*(pltpu.with_memory_space_constraint(value, pltpu.HBM) for value in operands))
     return pl.pallas_call(
         product_kernel,
-        in_specs=[vmem] * 3,
+        in_specs=[vmem] * 5,
         out_specs=hbm,
         out_shape=jax.ShapeDtypeStruct((height, width), jnp.float32),
         scratch_shapes=[
             pltpu.VMEM((height, width), jnp.float32),
-            pltpu.VMEM((192, width), jnp.bfloat16),
+            pltpu.VMEM((256, width), jnp.bfloat16),
             dma((ROWS,)),
         ],
         compiler_params=pltpu.CompilerParams(vmem_limit_bytes=32 * 2**20),
         name="product",
-    )(left.reshape(-1, LANES), right.reshape(-1, LANES), total)
+    )(left.reshape(-1, LANES), right.reshape(-1, LANES), *rest)
 
 
 def solution(mesh):

time: 31.2 us -> 30.1 us (0.965)
  Pallas kernels: 30.7 us -> 29.8 us
    pallas_call x2, Pallas kernels: 30.7 us -> 29.8 us  [the longest x1 26.1 us: body(): pl.pallas_call(gather_kernel, in_specs=[hbm] * 6, out_specs=[vmem] * 5, o...]
where the time goes in v5:
time: 30.1 us; the launch traced here: 29.8 us
  Pallas kernels  29.8 us (99%)
    pallas_call x1, Pallas kernels, body(): pl.pallas_call(gather_kernel, in_specs=[hbm] * 6, out_specs=[vmem] * 5, o...  26.1 us
    pallas_call x1, Pallas kernels, body(): pl.pallas_call(product_kernel, in_specs=[vmem] * 5, out_specs=hbm, out_sh...  3.72 us

profile of v5, /device:TPU:0, one launch (start us, length us, event | category | flops | bytes accessed | tf_op | source)
XLA Modules:
  0.0 29.8 jit_solution(4741116609999634149)
XLA Ops:
  0.0 26.1 %gather.1 = (f32[4,4,2,2,4,2,8,128]{7,6,5,4,3,2,1,0:T(8,128)S(1)}, f32[4,2,4,2,4,8,128]{6,5,4,3,2,1,0:T(8,128)S(1)}, f32[2048,1024]{1,0:T(8,128)S(1)}, bf16[8,64...) custom-call(s32[2]{0:T(128)} %counts.1, bf16[2,2400,256]{2,1,0:T(8,128)(2,1)} %features.1, s32[2,4,2400]{2,1,0:T(4,128)} %ids.1, ...), custom_call_target="tpu_custom_call" | custom-call | tf_op jit(solution)/shard_map/gather/pallas_call | solution.py:295
  26.1 3.7 %product.1 = f32[2048,1024]{1,0:T(8,128)} custom-call(f32[4096,128]{1,0:T(8,128)S(1)} %bitcast.2, f32[2048,128]{1,0:T(8,128)S(1)} %bitcast.3, f32[2048,1024]{1,0:T(8,128)S(1)} %get-tuple-element.12.total, bf16[8,64,256]{2,1,0:T(8,128)(2,1)S(1)} %get-tuple-element.13.spare_rows, bf16[64,1024]{1,0:T(8,128)(2,1)S(1)} %get-tuple-element.14.spare_columns), custom_call_target="tpu_custom_call" | custom-call | tf_op jit(solution)/shard_map/product/pallas_call | solution.py:324

commit v6 on v5

--- a/solution.py
+++ b/solution.py
@@ -139,19 +139,21 @@
             target = left.at[0, j, :, k, PLACE[BACK[u]]]
             put(left.at[0, j, :, k, 0], target, u_send.at[k], u_recv.at[k, j], along(k, u, 0))
 
-    onward = {}
+    def second(k, j, slots):
+        for n, turn in enumerate((1, -1)):
+            target = left.at[PLACE[-turn], j, :, k, slots]
+            put(left.at[0, j, :, k, slots], target, v_send.at[k], v_recv.at[k, j, n], along(k, 0, turn))
+
+    def go_own(k, j):
+        second(k, j, pl.ds(0, 1))
 
     def go_v(k, j):
         wait(left.at[0, j, :, k, pl.ds(1, 3)], u_recv.at[k, j])
-        for n, turn in enumerate((1, -1)):
-            target = left.at[PLACE[-turn], j, :, k]
-            onward[k, j, n] = put(
-                left.at[0, j, :, k], target, v_send.at[k], v_recv.at[k, j, n], along(k, 0, turn)
-            )
+        second(k, j, pl.ds(1, 3))
 
     def relay(k, j):
         for n, turn in enumerate((1, -1)):
-            onward[k, j, n].wait_recv()
+            wait(left.at[PLACE[-turn], j, :, k], v_recv.at[k, j, n])
             source = left.at[PLACE[-turn], j, :, k, pl.ds(2 * n, 2)]
             target = left.at[PLACE[2], j, :, k, pl.ds(2 * n, 2)]
             put(source, target, r_send.at[k], r_recv.at[k], along(k, 0, turn))
@@ -193,11 +195,11 @@
 
     aggregate(0)
     pl.semaphore_wait(barrier, len(plane + column))
+    row_pieces(0)
     column_pieces(0)
-    row_pieces(0)
     aggregate(1)
+    row_pieces(1)
     column_pieces(1)
-    row_pieces(1)
     for k in range(2):
         go_u(k, 0)
     for k in range(2):
@@ -206,6 +208,14 @@
         go_u(k, 2)
     for k in range(2):
         go_u(k, 3)
+    for k in range(2):
+        go_own(k, 0)
+    for k in range(2):
+        go_own(k, 1)
+    for k in range(2):
+        go_own(k, 2)
+    for k in range(2):
+        go_own(k, 3)
     wait(right.at[0, 0], c_recv.at[0])
     spread = {
         dz: put(

time: 30.1 us -> 30 us (level)
  no operation moved by 1% of the time
where the time goes in v6:
time: 30 us; the launch traced here: 29.7 us
  Pallas kernels  29.7 us (99%)
    pallas_call x1, Pallas kernels, body(): pl.pallas_call(gather_kernel, in_specs=[hbm] * 6, out_specs=[vmem] * 5, o...  26 us
    pallas_call x1, Pallas kernels, body(): pl.pallas_call(product_kernel, in_specs=[vmem] * 5, out_specs=hbm, out_sh...  3.72 us

profile of v6, /device:TPU:0, one launch (start us, length us, event | category | flops | bytes accessed | tf_op | source)
XLA Modules:
  0.0 29.7 jit_solution(11749282416300350018)
XLA Ops:
  0.0 26.0 %gather.1 = (f32[4,4,2,2,4,2,8,128]{7,6,5,4,3,2,1,0:T(8,128)S(1)}, f32[4,2,4,2,4,8,128]{6,5,4,3,2,1,0:T(8,128)S(1)}, f32[2048,1024]{1,0:T(8,128)S(1)}, bf16[8,64...) custom-call(s32[2]{0:T(128)} %counts.1, bf16[2,2400,256]{2,1,0:T(8,128)(2,1)} %features.1, s32[2,4,2400]{2,1,0:T(4,128)} %ids.1, ...), custom_call_target="tpu_custom_call" | custom-call | tf_op jit(solution)/shard_map/gather/pallas_call | solution.py:305
  26.0 3.7 %product.1 = f32[2048,1024]{1,0:T(8,128)} custom-call(f32[4096,128]{1,0:T(8,128)S(1)} %bitcast.2, f32[2048,128]{1,0:T(8,128)S(1)} %bitcast.3, f32[2048,1024]{1,0:T(8,128)S(1)} %get-tuple-element.12.total, bf16[8,64,256]{2,1,0:T(8,128)(2,1)S(1)} %get-tuple-element.13.spare_rows, bf16[64,1024]{1,0:T(8,128)(2,1)S(1)} %get-tuple-element.14.spare_columns), custom_call_target="tpu_custom_call" | custom-call | tf_op jit(solution)/shard_map/product/pallas_call | solution.py:334

commit v7 on v6

--- a/solution.py
+++ b/solution.py
@@ -165,8 +165,8 @@
     flat_right = right.reshape(-1, LANES)
     flat_left = left.reshape(-1, LANES)
 
-    def stack_rows(v):
-        for k in range(ROWS):
+    def stack_rows(v, clusters=range(ROWS)):
+        for k in clusters:
             values = [flat_left[pl.ds(v * 1024 + half * ROWS + k, 64, stride=16), :] for half in range(2)]
             top, rest = split(jnp.concatenate(values, axis=1))
             stacked[k, v * 64 : (v + 1) * 64] = top
@@ -253,12 +253,12 @@
     stack_columns(1)
     twins[2].wait_recv()
     stack_columns(2)
-    stack_rows(1)
-    stack_rows(2)
     twins[3].wait_recv()
     stack_columns(3)
     fill.wait()
     for k in range(ROWS):
+        stack_rows(1, (k,))
+        stack_rows(2, (k,))
         total[k * DESC : (k + 1) * DESC] += lax.dot_general(
             stacked[k], factor[...], DIMS, preferred_element_type=jnp.float32
         )

time: 30 us -> 29.9 us (level)
  no operation moved by 1% of the time
where the time goes in v7:
time: 29.9 us; the launch traced here: 29.7 us
  Pallas kernels  29.7 us (99%)
    pallas_call x1, Pallas kernels, body(): pl.pallas_call(gather_kernel, in_specs=[hbm] * 6, out_specs=[vmem] * 5, o...  26 us
    pallas_call x1, Pallas kernels, body(): pl.pallas_call(product_kernel, in_specs=[vmem] * 5, out_specs=hbm, out_sh...  3.72 us

profile of v7, /device:TPU:0, one launch (start us, length us, event | category | flops | bytes accessed | tf_op | source)
XLA Modules:
  0.0 29.7 jit_solution(10806836723892421557)
XLA Ops:
  0.0 26.0 %gather.1 = (f32[4,4,2,2,4,2,8,128]{7,6,5,4,3,2,1,0:T(8,128)S(1)}, f32[4,2,4,2,4,8,128]{6,5,4,3,2,1,0:T(8,128)S(1)}, f32[2048,1024]{1,0:T(8,128)S(1)}, bf16[8,64...) custom-call(s32[2]{0:T(128)} %counts.1, bf16[2,2400,256]{2,1,0:T(8,128)(2,1)} %features.1, s32[2,4,2400]{2,1,0:T(4,128)} %ids.1, ...), custom_call_target="tpu_custom_call" | custom-call | tf_op jit(solution)/shard_map/gather/pallas_call | solution.py:305
  26.0 3.7 %product.1 = f32[2048,1024]{1,0:T(8,128)} custom-call(f32[4096,128]{1,0:T(8,128)S(1)} %bitcast.2, f32[2048,128]{1,0:T(8,128)S(1)} %bitcast.3, f32[2048,1024]{1,0:T(8,128)S(1)} %get-tuple-element.12.total, bf16[8,64,256]{2,1,0:T(8,128)(2,1)S(1)} %get-tuple-element.13.spare_rows, bf16[64,1024]{1,0:T(8,128)(2,1)S(1)} %get-tuple-element.14.spare_columns), custom_call_target="tpu_custom_call" | custom-call | tf_op jit(solution)/shard_map/product/pallas_call | solution.py:334
